TPU v7x, 32 devices: a whole 2x2x4 slice. The times are simulated.
32 devices in a mesh: groups: 2 (over x), pool: 8 (over z, y), tensor: 2 (over core).
Axes of the slice: x: 2, y: 2, z: 4, core: 2. Of those that a mesh axis runs over, the one named last changes fastest.
Arguments:
- hidden: bfloat16 [16384, 8192], P(('groups', 'pool'), 'tensor'), parts along dimension 0, may hold values from -300 to 300
- norm_gain: bfloat16 [8192], P('tensor'), may hold values from 0.099609375 to 1.8984375
- key_value_weight: bfloat16 [8192, 2, 512], P('tensor', None, 'pool'), may hold values from -0.0625 to 0.0625
- key_value_bias: bfloat16 [2, 512], P(None, 'tensor'), may hold values from -3 to 3
- stored_page_pool: bfloat16 [64, 128, 2, 512], P(('groups', 'pool'), None, None, 'tensor'), parts along dimension 0, may hold values from -6 to 6
- page_request: int32 [64], P(('groups', 'pool')), parts along dimension 0, may hold values from 0 to 7, as said below
- prefix_len: int32 [16], P(('groups', 'pool')), parts along dimension 0, may hold values from 1 to 1024, as said below
- queries: bfloat16 [512, 4096], P(('groups', 'pool'), 'tensor'), parts along dimension 0, may hold values from -20 to 20
- new_key_value: bfloat16 [512, 2, 512], P(('groups', 'pool'), None, 'tensor'), parts along dimension 0, may hold values from -6 to 6
Outputs:
- attended: bfloat16 [512, 4096], P(('groups', 'pool'), 'tensor'), parts along dimension 0
There are 2 independent parts, one for each index of `groups`. A program takes and returns all parts, laid end to end along the dimension named above; an argument that names none is the same for every part. Nothing has to cross between parts.
Inputs may be any that keep to these rules, and one draw needn't show every extreme that they name: `page_request`: each device's 4 pages name requests of the group; no device stores more than 1 pages of one request; in every draw one request has exactly 1 pages on every device. `prefix_len`: some request has the whole 1024 rows.
All inputs are finite; a program needn't handle non-finite values.
Results may differ from a plain program's by a relative error of at most 0.015.
Values may be sent and summed in bfloat16 or wider, within the bound.
A program may use at most 128 MiB of HBM per device.

v0:
```python
import math

import jax
import jax.numpy as jnp
from jax import lax
from jax.sharding import PartitionSpec as P

MODEL_WIDTH = 8192
HEADS_PER_GROUP = 8
HEAD_WIDTH = 128
CAP = 1


rope_base = 1000000.0
epsilon = 1e-06


def apply_rotation(key_portion, token_positions):
    half_dim = key_portion.shape[-1] // 2
    frequency = rope_base ** (
        -(jnp.arange(half_dim, dtype=jnp.float32) * 2.0 / key_portion.shape[-1])
    )
    angles = token_positions.astype(jnp.float32)[:, None] * frequency[None, :]
    cosine = jnp.cos(angles)[:, None, :]
    sine_part = jnp.sin(angles)[:, None, :]
    lead_half = key_portion[..., :half_dim]
    tail_half = key_portion[..., half_dim:]
    return jnp.concatenate(
        [lead_half * cosine - tail_half * sine_part, tail_half * cosine + lead_half * sine_part],
        axis=-1,
    )


def absorb(running, query_heads, key_portion, value_part, visible):
    highest, mass_sum, weighted = running
    scores = jnp.einsum(
        "hgqd,khd->hgqk", query_heads, key_portion, preferred_element_type=jnp.float32
    ) * query_heads.shape[-1] ** (-0.5)
    scores = jnp.where(visible, scores, -jnp.inf)
    new_high = jnp.maximum(highest, jnp.max(scores, axis=-1))
    anchor = jnp.where(jnp.isfinite(new_high), new_high, 0.0)
    prob_rows = jnp.exp(scores - anchor[..., None])
    factor = jnp.exp(highest - anchor)
    mass_sum = mass_sum * factor + jnp.sum(prob_rows, axis=-1)
    weighted = weighted * factor[..., None] + jnp.einsum(
        "hgqk,khd->hgqd",
        prob_rows.astype(jnp.bfloat16),
        value_part,
        preferred_element_type=jnp.float32,
    )
    return (new_high, mass_sum, weighted)


def local(
    hidden,
    norm_gain,
    key_value_weight,
    key_value_bias,
    stored_page_pool,
    page_request,
    prefix_len,
    queries,
    new_key_value,
):
    row_count = hidden.shape[0]
    wide_hidden = hidden.astype(jnp.float32)
    scaled_scores = (wide_hidden * norm_gain.astype(jnp.float32)[None, :]).astype(jnp.bfloat16)
    local_squares = jnp.sum(wide_hidden * wide_hidden, axis=1)
    piece = lax.all_gather(key_value_weight, "pool", axis=2, tiled=True)
    width_part = piece.shape[2]
    product = jnp.dot(
        scaled_scores,
        piece.reshape(piece.shape[0], 2 * width_part),
        preferred_element_type=jnp.float32,
    )
    partial_value = product.reshape(row_count, 2, width_part)
    squares = lax.psum(local_squares, "tensor")
    projected_hidden = lax.psum_scatter(
        partial_value.astype(jnp.bfloat16), "tensor", scatter_dimension=2, tiled=True
    ).astype(jnp.float32)
    inverse_frequency = lax.rsqrt(squares / MODEL_WIDTH + epsilon)
    local_heads = projected_hidden.shape[2] // HEAD_WIDTH
    kv_rows = (
        inverse_frequency[:, None, None] * projected_hidden
        + key_value_bias.astype(jnp.float32)[None]
    )
    kv_rows = kv_rows.reshape(row_count, 2, local_heads, HEAD_WIDTH)
    token_positions = jnp.arange(row_count, dtype=jnp.int32)
    restored_prefix_keys = apply_rotation(kv_rows[:, 0], token_positions).astype(jnp.bfloat16)
    restored_prefix_values = kv_rows[:, 1].astype(jnp.bfloat16)
    fresh_count = queries.shape[0]
    query_heads = queries.reshape(fresh_count, local_heads, HEADS_PER_GROUP, HEAD_WIDTH).transpose(
        1, 2, 0, 3
    )
    fresh_keys = new_key_value[:, 0].reshape(fresh_count, local_heads, HEAD_WIDTH)
    fresh_values = new_key_value[:, 1].reshape(fresh_count, local_heads, HEAD_WIDTH)
    prefix_ok = token_positions < prefix_len[0]
    causal = jnp.arange(fresh_count)[None, :] <= jnp.arange(fresh_count)[:, None]
    visible = jnp.concatenate(
        [jnp.broadcast_to(prefix_ok[None, :], (fresh_count, row_count)), causal], axis=1
    )
    start_state = (
        jnp.full((local_heads, HEADS_PER_GROUP, fresh_count), -jnp.inf, jnp.float32),
        jnp.zeros((local_heads, HEADS_PER_GROUP, fresh_count), jnp.float32),
        jnp.zeros((local_heads, HEADS_PER_GROUP, fresh_count, HEAD_WIDTH), jnp.float32),
    )
    running = absorb(
        start_state,
        query_heads,
        jnp.concatenate([restored_prefix_keys, fresh_keys], axis=0),
        jnp.concatenate([restored_prefix_values, fresh_values], axis=0),
        visible,
    )
    page_count = page_request.shape[0]
    page_index = jnp.arange(page_count)
    same_request = (page_request[:, None] == page_request[None, :]) & (
        page_index[None, :] < page_index[:, None]
    )
    slot_rank = jnp.sum(same_request.astype(jnp.int32), axis=1)
    pool_size = lax.axis_size("pool")
    page_len = stored_page_pool.shape[1]
    outgoing = (
        jnp.zeros((pool_size, CAP) + stored_page_pool.shape[1:], jnp.bfloat16)
        .at[page_request, slot_rank]
        .set(stored_page_pool)
    )
    occupied = jnp.zeros((pool_size, CAP), jnp.bfloat16).at[page_request, slot_rank].set(1.0)
    arrived, present = (
        lax.all_to_all(outgoing, "pool", split_axis=0, concat_axis=0, tiled=True),
        lax.all_to_all(occupied, "pool", split_axis=0, concat_axis=0, tiled=True),
    )
    slot_total_count = pool_size * CAP
    per_block = math.gcd(slot_total_count, max(1, 1024 // page_len))
    grouped = arrived.reshape(
        slot_total_count // per_block, per_block * page_len, 2, local_heads, HEAD_WIDTH
    )
    live_keys = (
        jnp.repeat(present.reshape(slot_total_count // per_block, per_block), page_len, axis=1)
        > 0.5
    )

    def visit_block(carried, scan_item):
        page_block, is_live = scan_item
        return (
            absorb(carried, query_heads, page_block[:, 0], page_block[:, 1], is_live[None, :]),
            None,
        )

    running, unused = lax.scan(visit_block, running, (grouped, live_keys))
    highest, mass_sum, weighted = running
    attended = weighted / mass_sum[..., None]
    return attended.transpose(2, 0, 1, 3).reshape(fresh_count, -1).astype(jnp.bfloat16)


def solution(mesh):
    return jax.shard_map(
        local,
        mesh=mesh,
        in_specs=(
            P(("groups", "pool"), "tensor"),
            P("tensor"),
            P("tensor", None, "pool"),
            P(None, "tensor"),
            P(("groups", "pool"), None, None, "tensor"),
            P(("groups", "pool")),
            P(("groups", "pool")),
            P(("groups", "pool"), "tensor"),
            P(("groups", "pool"), None, "tensor"),
        ),
        out_specs=P(("groups", "pool"), "tensor"),
        check_vma=False,
    )
```

profile of v0, /device:TPU:1, one launch (start us, length us, event | category | flops | bytes accessed | tf_op | source)
XLA Modules:
  0.0 217.9 jit_solution(14483780870461762190)
XLA Ops:
  6.5 0.0 all-gather.2.cloned.1.call-start
  6.5 0.7 all-gather.2.cloned.1.call-update
  7.3 0.0 reduce-scatter.2.cloned.1.call-start
  7.3 0.7 convert_element_type.53
  8.0 128.2 %all-gather.2.cloned.1.call-done = bf16[4096,2,512]{0,2,1:T(8,128)(2,1)} async-done(((bf16[4096,2,64]{0,2,1:T(8,128)(2,1)}), bf16[4096,2,512]{0,2,1:T(8,128)(2,1)}) %all-gather.2.cloned.1.call-update) | async-done | bytes 8388624 | tf_op jit(solution)/shard_map/all_gather | solution.py:69
  136.2 14.8 %fusion.12 = bf16[1024,2,512]{2,0,1:T(8,128)(2,1)} fusion(bf16[4096,2,512]{0,2,1:T(8,128)(2,1)} %all-gather.2.cloned.1.call-done, bf16[1024,4096]{1,0:T(8,128)(2,1)} %param.9, f32[4096]{0:T(1024)S(1)} %convert_element_type.53), kind=kOutput, calls=%fused_computation.21 | convolution fusion | flops 8603566080 | bytes 18890752 | tf_op jit(solution)/shard_map/dot_general | solution.py:71
  151.0 0.0 reduce-scatter.2.cloned.1.call-update
  151.0 0.6 copy-done.7
  151.6 0.2 convert_reduce_fusion
  151.8 0.6 scatter_custom_fusion
  152.4 0.7 copy.53
  153.1 3.3 %all-to-all-start = ((bf16[8,1,1]{2,1,0:T(2,128)(2,1)}), bf16[8,1,1]{2,1,0:T(2,128)(2,1)S(1)}, u32[]{:S(2)}, u32[]{:S(2)}) async-start(bf16[8,1,1]{2,1,0:T(2,128)(2,1)} %copy.53), calls=%async_computation.1 | async-start | bytes 8192 | tf_op jit(solution)/shard_map/all_to_all | solution.py:130
  157.1 0.0 copy-done.3
  157.1 0.1 copy.54
  157.2 1.1 broadcast.162
  158.3 2.5 %scatter_fusion = bf16[8,128,2,256]{3,1,2,0:T(8,128)(2,1)} fusion(bf16[8,128,2,256]{3,1,2,0:T(8,128)(2,1)} %broadcast.162, s32[4]{0:T(128)S(1)} %fusion.65, bf16[4,128,2,256]{3,1,2,0:T(8,128)(2,1)S(1)} %copy.54), kind=kCustom, calls=%fused_computation.1 | custom fusion | bytes 1572880 | tf_op jit(solution)/shard_map/scatter | solution.py:125
  160.9 5.1 %fusion = f32[1024]{0:T(1024)S(1)} fusion(bf16[1024,4096]{1,0:T(8,128)(2,1)} %param.9), kind=kLoop, calls=%fused_computation.4 | loop fusion | flops 12581888 | bytes 8392704 | tf_op jit(solution)/shard_map/reduce_sum | solution.py:68
  166.0 0.0 copy-start.5
  166.0 0.0 copy-start.4
  166.0 0.0 all-to-all-done
  166.0 5.5 %all-to-all-start.1 = ((bf16[8,1,128,2,256]{4,2,3,1,0:T(8,128)(2,1)}), bf16[8,1,128,2,256]{4,2,3,1,0:T(8,128)(2,1)S(1)}, u32[]{:S(2)}, u32[]{:S(2)}) async-start(bf16[8,1,128,2,256]{4,2,3,1,0:T(8,128)(2,1)} %bitcast.21), calls=%async_computation.2 | async-start | bytes 2097152 | tf_op jit(solution)/shard_map/all_to_all | solution.py:129
  171.5 3.7 %psum.7 = f32[1024]{0:T(1024)S(1)} all-reduce(f32[1024]{0:T(1024)S(1)} %fusion), channel_id=1, replica_groups=mesh['groups'=2,'pool'=8,'tensor'=2] {'tensor'}, use_global_device_ids=true, to_apply=%region_1.0 | all-reduce | flops 1024 | bytes 8192 | tf_op jit(solution)/shard_map/psum | solution.py:77
  175.3 0.1 slice_reduce_fusion
  175.4 3.1 %multiply_cosine_fusion = (f32[1024,64]{1,0:T(8,128)}, f32[1024,64]{1,0:T(8,128)}) fusion(f32[64]{0:T(128)S(1)} %negate_power_fusion, f32[1024]{0:T(1024)S(1)} %iota_convert_fusion), kind=kLoop, calls=%fused_computation.42 | loop fusion | flops 65536 | bytes 528640 | tf_op jit(solution)/shard_map/cos | solution.py:24
  178.5 0.2 compare_reduce_fusion
  178.8 0.1 broadcast_bitcast_fusion
  178.9 17.0 %all-to-all-done.1 = bf16[8,1,128,2,256]{4,2,3,1,0:T(8,128)(2,1)S(1)} async-done(((bf16[8,1,128,2,256]{4,2,3,1,0:T(8,128)(2,1)}), bf16[8,1,128,2,256]{4,2,3,1,0:T(8,128)(2,1)S(1)}, u32[]{:S(2)}, u32[]{:S(2)}) %all-to-all-start.1) | async-done | bytes 1048608 | tf_op jit(solution)/shard_map/all_to_all | solution.py:129
  195.9 0.7 copy.56
  196.7 0.5 squeeze.24
  197.2 0.5 bitcast_reduce_fusion
  197.7 0.0 reduce-scatter.2.cloned.1.call-done
  197.7 2.8 %multiply_add_fusion = f32[1024,2,256]{2,0,1:T(8,128)} fusion(bf16[1024,2,256]{2,0,1:T(8,128)(2,1)} %reduce-scatter.2.cloned.1.call-done, f32[2,256]{1,0:T(2,128)S(1)} %convert_element_type.57, f32[1024]{0:T(1024)S(1)} %add_rsqrt_fusion), kind=kLoop, calls=%fused_computation.18 | loop fusion | flops 1572864 | bytes 3151872 | tf_op jit(solution)/shard_map/add | solution.py:84
  200.5 3.3 %reshape.146 = f32[1024,2,2,128]{3,2,0,1:T(2,128)} reshape(f32[1024,2,256]{2,0,1:T(8,128)} %multiply_add_fusion) | data formatting | bytes 4194304 | tf_op jit(solution)/shard_map/reshape | solution.py:87
  203.8 1.2 slice-done
  205.0 0.1 copy.92
  205.1 0.1 copy-done.1
  205.2 0.2 copy-done.2
  205.3 0.5 subtract_convert_fusion
  205.8 0.8 fusion.73
  206.6 0.5 fusion.17
  207.1 0.6 convolution_bitcast_fusion
  207.7 1.0 copy-done
  208.7 0.4 slice.42
  209.1 0.1 copy.93
  209.1 0.5 fusion.10
  209.7 0.7 fusion.37
  210.3 0.1 copy.59
  210.4 0.7 copy.94
  (25 shorter events, 0.1 us)
Async XLA Ops:
  6.5 129.6 %all-gather.2.cloned.1.call-start = ((), (), s32[]{:S(2)}) async-start(), calls=%async_computation.3 | async-start | bytes 9437184 | tf_op jit(solution)/shard_map/all_gather | solution.py:69
  7.3 190.4 %reduce-scatter.2.cloned.1.call-start = ((), (), s32[]{:S(2)}) async-start(), calls=%async_computation.4 | async-start | bytes 3145728 | tf_op jit(solution)/shard_map/reduce_scatter | solution.py:78
  151.0 0.7 copy-start.7
  151.0 6.1 %copy-start.3 = (bf16[4,128,2,256]{3,2,1,0:T(2,128)(2,1)S(1)}, bf16[4,128,2,256]{3,2,1,0:T(2,128)(2,1)}, u32[]{:S(2)}) copy-start(bf16[4,128,2,256]{3,2,1,0:T(2,128)(2,1)} %param.13) | copy-start | bytes 1572868
  153.1 12.9 %all-to-all-start = ((bf16[8,1,1]{2,1,0:T(2,128)(2,1)}), bf16[8,1,1]{2,1,0:T(2,128)(2,1)S(1)}, u32[]{:S(2)}, u32[]{:S(2)}) async-start(bf16[8,1,1]{2,1,0:T(2,128)(2,1)} %copy.53), calls=%async_computation.1 | async-start | bytes 8192 | tf_op jit(solution)/shard_map/all_to_all | solution.py:130
  165.9 9.3 %copy-start.6 = (bf16[2,256]{1,0:T(2,128)(2,1)S(1)}, bf16[2,256]{1,0:T(2,128)(2,1)}, u32[]{:S(2)}) copy-start(bf16[2,256]{1,0:T(2,128)(2,1)} %param.12) | copy-start | bytes 3076
  166.0 9.3 %copy-start.5 = (bf16[32,2048]{1,0:T(8,128)(2,1)S(1)}, bf16[32,2048]{1,0:T(8,128)(2,1)}, u32[]{:S(2)}) copy-start(bf16[32,2048]{1,0:T(8,128)(2,1)} %param.16) | copy-start | bytes 393220
  166.0 9.3 %copy-start.4 = (bf16[32,2,256]{2,1,0:T(2,128)(2,1)S(1)}, bf16[32,2,256]{2,1,0:T(2,128)(2,1)}, u32[]{:S(2)}) copy-start(bf16[32,2,256]{2,1,0:T(2,128)(2,1)} %param.17) | copy-start | bytes 98308
  166.0 29.9 %all-to-all-start.1 = ((bf16[8,1,128,2,256]{4,2,3,1,0:T(8,128)(2,1)}), bf16[8,1,128,2,256]{4,2,3,1,0:T(8,128)(2,1)S(1)}, u32[]{:S(2)}, u32[]{:S(2)}) async-start(bf16[8,1,128,2,256]{4,2,3,1,0:T(8,128)(2,1)} %bitcast.21), calls=%async_computation.2 | async-start | bytes 2097152 | tf_op jit(solution)/shard_map/all_to_all | solution.py:129
  203.8 1.2 slice-start
  203.8 1.4 copy-start.1
  203.8 1.5 copy-start.2
  207.1 1.6 copy-start
Sparse Core Ops, SparseCore 0:
  9.5 126.5 all-gather.1
  151.1 8.5 reduce-scatter.1
where the time goes:
time: 221 us; the launch traced here: 218 us
  waiting for transfers between devices  146 us (66%)
  matrix products  17.3 us (8%)
  between operations  14.3 us (6%)
  local copies, waits for them, and re-layouts  14.2 us (6%)
  other arithmetic  13.6 us (6%)
  starting transfers between devices  8.87 us (4%)
  blocking collectives  3.7 us (2%)
    all_gather x1, waiting for transfers between devices, local(): piece = lax.all_gather(key_value_weight, 'pool', axis=2, tiled=True)  128 us
    all_to_all x1, waiting for transfers between devices, local(): lax.all_to_all(outgoing, 'pool', split_axis=0, concat_axis=0, tiled=True)  17 us
    dot_general x1, matrix products, local(): jnp.dot(scaled_scores, piece.reshape(piece.shape[0], 2 * width_part), pre...  14.8 us
    all_to_all x1, starting transfers between devices, local(): lax.all_to_all(outgoing, 'pool', split_axis=0, concat_axis=0, tiled=True)  5.52 us
    reduce_sum x1, other arithmetic, local(): local_squares = jnp.sum(wide_hidden * wide_hidden, axis=1)  5.07 us
  transfers between devices with their start and end apart: 4, of which 2 were waited for; matrix products, arithmetic and copies ran while one was open for 8% of the time, Pallas kernels for 0%

commit v1 on v0

--- a/solution.py
+++ b/solution.py
@@ -1,8 +1,11 @@
 import math
 
+import numpy as np
 import jax
 import jax.numpy as jnp
 from jax import lax
+from jax.experimental import pallas as pl
+from jax.experimental.pallas import tpu as pltpu
 from jax.sharding import PartitionSpec as P
 
 MODEL_WIDTH = 8192
@@ -13,6 +16,7 @@
 
 rope_base = 1000000.0
 epsilon = 1e-06
+MESH = pl.DeviceIdType.MESH
 
 
 def apply_rotation(key_portion, token_positions):
@@ -152,9 +156,430 @@
     return attended.transpose(2, 0, 1, 3).reshape(fresh_count, -1).astype(jnp.bfloat16)
 
 
+NSUB = 2
+MASKED = -1e30
+FLAG_ROWS = 16
+
+
+def rotation_tables(row_count):
+    half = HEAD_WIDTH // 2
+    frequency = rope_base ** (-(np.arange(half, dtype=np.float64) * 2.0 / HEAD_WIDTH))
+    angles = np.arange(row_count, dtype=np.float64)[:, None] * frequency[None, :]
+    cosine, sine = np.cos(angles), np.sin(angles)
+    return (
+        np.concatenate([cosine, cosine], axis=1).astype(np.float32),
+        np.concatenate([-sine, sine], axis=1).astype(np.float32),
+    )
+
+
+def fused_kernel(
+    w_ref, h_ref, gain_ref, bias_ref, page_ref, req_ref, plen_ref, q_ref, nkv_ref, cos_ref, sin_ref,
+    out_ref,
+    wbuf, hraw, hs, accs, psend_buf, precv_buf, ss_send, ss_recv, pout, pin, qbuf, kbuf, vbuf, obuf,
+    m_st, l_st, a_st,
+    h_sem, own_sem, page_self_sem, w_send, w_recv, part_send, part_recv, ss_sems, pg_send, pg_recv,
+):
+    f32, bf16 = jnp.float32, jnp.bfloat16
+    rows, half_width = hs.shape[1], hs.shape[2]
+    sub = half_width // NSUB
+    x = lax.axis_index("groups")
+    me = lax.axis_index("pool")
+    t = lax.axis_index("tensor")
+    z, y = me // 2, lax.rem(me, 2)
+    ox, oy, ot = 1 - x, 1 - y, 1 - t
+    depth = 4
+
+    def device(g, p, c):
+        return {"groups": g, "pool": p, "tensor": c}
+
+    x_peer = device(ox, me, t)
+    y_peer = device(x, z * 2 + oy, t)
+    up_peer = device(x, jnp.minimum(z + 1, depth - 1) * 2 + y, t)
+    down_peer = device(x, jnp.maximum(z - 1, 0) * 2 + y, t)
+    t_peer = device(x, me, ot)
+    has_up, has_down = z < depth - 1, z > 0
+
+    blocks = h_sem.shape[0]
+    block_rows = rows // blocks
+
+    def hidden_copy(b):
+        window = pl.ds(b * block_rows, block_rows)
+        return pltpu.make_async_copy(h_ref.at[window], hraw.at[window], h_sem.at[b])
+
+    for b in range(blocks):
+        hidden_copy(b).start()
+    own_copy = pltpu.make_async_copy(w_ref, wbuf.at[me], own_sem)
+    own_copy.start()
+
+    barrier = pltpu.get_barrier_semaphore()
+    for o in range(1, 8):
+        pl.semaphore_signal(
+            barrier, inc=1, device_id=device(x, lax.rem(me + o, 8), t), device_id_type=MESH
+        )
+    pl.semaphore_signal(barrier, inc=1, device_id=x_peer, device_id_type=MESH)
+    pl.semaphore_signal(barrier, inc=1, device_id=t_peer, device_id_type=MESH)
+    pl.semaphore_wait(barrier, 9)
+
+    started = []
+
+    def window(h, s):
+        return pl.ds(pl.multiple_of(h * half_width + s * sub, sub), sub)
+
+    def piece(slot, h, s):
+        return wbuf.at[slot, window(h, s), :]
+
+    def copy_of(way, slot, h, s, peer, own=False):
+        source = w_ref.at[window(h, s), :] if own else piece(slot, h, s)
+        return pltpu.make_async_remote_copy(
+            src_ref=source,
+            dst_ref=piece(slot, h, s),
+            send_sem=w_send.at[way, slot, h, s],
+            recv_sem=w_recv.at[slot, h, s],
+            device_id=peer,
+            device_id_type=MESH,
+        )
+
+    def send(way, slot, h, s, peer, cond=None, own=False):
+        copy = copy_of(way, slot, h, s, peer, own)
+        started.append((cond, copy))
+        if cond is None:
+            copy.start()
+        else:
+            pl.when(cond)(copy.start)
+
+    def arrive(slot, h, s):
+        copy_of(2, slot, h, s, x_peer).wait_recv()
+
+    for s in range(NSUB):
+        send(0, me, x, s, up_peer, has_up, own=True)
+        send(1, me, x, s, down_peer, has_down, own=True)
+        send(3, me, x, s, y_peer, own=True)
+
+    gain = gain_ref[...].astype(f32)
+
+    step_rows = 16
+
+    def scale_block(b):
+        hidden_copy(b).wait()
+
+        @pl.loop(0, block_rows // step_rows)
+        def _(i):
+            at = pl.ds(pl.multiple_of(b * block_rows + i * step_rows, step_rows), step_rows)
+            wide = hraw[at, :].astype(f32)
+            scaled = (wide * gain).astype(bf16)
+            hs[0, at, :] = scaled[:, :half_width]
+            hs[1, at, :] = scaled[:, half_width:]
+            total = jnp.sum(wide * wide, axis=1, keepdims=True)
+            ss_send[at, :] = jnp.broadcast_to(total, (step_rows, HEAD_WIDTH))
+
+    for b in range(blocks // 2):
+        scale_block(b)
+
+    low = z < depth // 2
+    mirrored = jnp.where(low, z, depth - 1 - z)
+
+    def plane(k):
+        o = 1 - mirrored if k == 0 else k + 1
+        return jnp.where(low, o, depth - 1 - o)
+
+    def on_z(k):
+        zk = plane(k)
+        slot = zk * 2 + y
+        for s in range(NSUB):
+            arrive(slot, x, s)
+            if k < 2:
+                send(0, slot, x, s, up_peer, (zk < z) & has_up)
+                send(1, slot, x, s, down_peer, (zk > z) & has_down)
+            else:
+                send(0, slot, x, s, up_peer, (zk < z) & has_up)
+                send(1, slot, x, s, down_peer, (zk > z) & has_down)
+            send(2, slot, x, s, x_peer)
+            send(3, slot, x, s, y_peer)
+
+    def on_y(k):
+        slot = plane(k) * 2 + oy
+        for s in range(NSUB):
+            arrive(slot, x, s)
+            send(2, slot, x, s, x_peer)
+
+    def wait_all(slot, h):
+        for s in range(NSUB):
+            arrive(slot, h, s)
+
+    def multiply(slot, h, first):
+        @pl.loop(0, rows // 256)
+        def _(r):
+            at = pl.ds(pl.multiple_of(r * 256, 256), 256)
+            part = jnp.dot(
+                hs[h, at, :],
+                wbuf[slot, pl.ds(pl.multiple_of(h * half_width, half_width), half_width), :],
+                preferred_element_type=f32,
+            )
+            if first:
+                accs[slot, at, :] = part
+            else:
+                accs[slot, at, :] = accs[slot, at, :] + part
+
+    def part_copy(slot):
+        at = lax.rem(slot, 4)
+        return pltpu.make_async_remote_copy(
+            src_ref=psend_buf.at[at],
+            dst_ref=precv_buf.at[at],
+            send_sem=part_send.at[at],
+            recv_sem=part_recv.at[at],
+            device_id=t_peer,
+            device_id_type=MESH,
+        )
+
+    def complete(slot):
+        @pl.when(slot // 4 != t)
+        def _():
+            psend_buf[lax.rem(slot, 4)] = accs[slot].astype(bf16)
+            part_copy(slot).start()
+
+    page_len = page_ref.shape[1]
+
+    @pl.loop(0, 8)
+    def _(d):
+        taken = [(req_ref[i] == d).astype(f32) for i in range(page_ref.shape[0])]
+        for c in range(0, page_len, 32):
+            total = page_ref[0, c : c + 32, :].astype(f32) * taken[0]
+            for i in range(1, page_ref.shape[0]):
+                total = total + page_ref[i, c : c + 32, :].astype(f32) * taken[i]
+            pout[d, c : c + 32, :] = total.astype(bf16)
+        flag = taken[0] + taken[1] + taken[2] + taken[3]
+        pout[d, page_len:, :] = jnp.full((FLAG_ROWS, pout.shape[2]), 1.0, f32).astype(bf16) * flag.astype(bf16)
+
+    on_z(0)
+
+    for b in range(blocks // 2, blocks):
+        scale_block(b)
+    ss_copy = pltpu.make_async_remote_copy(
+        src_ref=ss_send,
+        dst_ref=ss_recv,
+        send_sem=ss_sems.at[0],
+        recv_sem=ss_sems.at[1],
+        device_id=t_peer,
+        device_id_type=MESH,
+    )
+    ss_copy.start()
+
+    self_page = pltpu.make_async_copy(pout.at[me], pin.at[me], page_self_sem)
+    self_page.start()
+
+    def page_copy(o, source, target):
+        return pltpu.make_async_remote_copy(
+            src_ref=pout.at[target],
+            dst_ref=pin.at[source],
+            send_sem=pg_send.at[o],
+            recv_sem=pg_recv.at[o],
+            device_id=device(x, target, t),
+            device_id_type=MESH,
+        )
+
+    page_sends = []
+    for o in range(1, 8):
+        copy = page_copy(o, me, lax.rem(me + o, 8))
+        copy.start()
+        page_sends.append(copy)
+
+    on_z(1)
+    own_copy.wait()
+    multiply(me, 0, True)
+    on_y(0)
+    on_z(2)
+    multiply(me, 1, False)
+    complete(me)
+    for s in range(NSUB):
+        send(3, me, ox, s, y_peer, own=True)
+    wait_all(z * 2 + oy, x)
+    multiply(z * 2 + oy, x, True)
+    multiply(plane(0) * 2 + y, x, True)
+    on_y(1)
+    wait_all(plane(0) * 2 + y, ox)
+    multiply(plane(0) * 2 + y, ox, False)
+    complete(plane(0) * 2 + y)
+    multiply(plane(0) * 2 + oy, x, True)
+    on_y(2)
+    multiply(plane(1) * 2 + y, x, True)
+    multiply(plane(1) * 2 + oy, x, True)
+    multiply(plane(2) * 2 + y, x, True)
+    multiply(plane(2) * 2 + oy, x, True)
+
+    heads = 2
+    fresh = q_ref.shape[0]
+    group_rows = HEADS_PER_GROUP * fresh
+    scale = HEAD_WIDTH ** (-0.5)
+    for j in range(heads):
+        for g in range(HEADS_PER_GROUP):
+            at = (j * HEADS_PER_GROUP + g) * HEAD_WIDTH
+            qbuf[j, g * fresh : (g + 1) * fresh, :] = q_ref[:, at : at + HEAD_WIDTH]
+
+    def inner(a, b):
+        return lax.dot_general(a, b, (((1,), (1,)), ((), ())), preferred_element_type=f32)
+
+    self_page.wait()
+    for o in range(1, 8):
+        page_copy(o, lax.rem(me + 8 - o, 8), me).wait_recv()
+    flags = jnp.concatenate(
+        [pin[i, page_len:, :HEAD_WIDTH].astype(f32)[:1, :] for i in range(8)], axis=1
+    )
+    for j in range(heads):
+        kc, vc = j * HEAD_WIDTH, (heads + j) * HEAD_WIDTH
+        query = qbuf[j]
+        near = inner(query, nkv_ref[:, kc : kc + HEAD_WIDTH]) * scale
+        row_at = lax.rem(lax.broadcasted_iota(jnp.int32, near.shape, 0), fresh)
+        near = jnp.where(lax.broadcasted_iota(jnp.int32, near.shape, 1) <= row_at, near, MASKED)
+        keys = pin[:, :page_len, kc : kc + HEAD_WIDTH].reshape(8 * page_len, HEAD_WIDTH)
+        values = pin[:, :page_len, vc : vc + HEAD_WIDTH].reshape(8 * page_len, HEAD_WIDTH)
+        far = jnp.where(flags > 0.5, inner(query, keys) * scale, MASKED)
+        high = jnp.maximum(
+            jnp.max(near, axis=1, keepdims=True), jnp.max(far, axis=1, keepdims=True)
+        )
+        near, far = jnp.exp(near - high), jnp.exp(far - high)
+        mass = jnp.sum(near, axis=1, keepdims=True) + jnp.sum(far, axis=1, keepdims=True)
+        m_st[j] = jnp.broadcast_to(high, (group_rows, HEAD_WIDTH))
+        l_st[j] = jnp.broadcast_to(mass, (group_rows, HEAD_WIDTH))
+        a_st[j] = jnp.dot(
+            near.astype(bf16), nkv_ref[:, vc : vc + HEAD_WIDTH], preferred_element_type=f32
+        ) + jnp.dot(far.astype(bf16), values, preferred_element_type=f32)
+
+    ss_copy.wait()
+
+    @pl.loop(0, rows // 128)
+    def _(r):
+        at = pl.ds(pl.multiple_of(r * 128, 128), 128)
+        ss_send[at, :] = lax.rsqrt((ss_send[at, :] + ss_recv[at, :]) / MODEL_WIDTH + epsilon)
+
+    half = HEAD_WIDTH // 2
+
+    def finish(j):
+        slot = (2 * t + j) * 2
+        for c in range(2):
+            part_copy(slot + c).wait_recv()
+        bias = jnp.where(j == 0, bias_ref[:, :HEAD_WIDTH].astype(f32), bias_ref[:, HEAD_WIDTH:].astype(f32))
+
+        @pl.loop(0, rows // 128)
+        def _(r):
+            at = pl.ds(pl.multiple_of(r * 128, 128), 128)
+            lead = accs[slot, at, :] + precv_buf[2 * j, at, :].astype(f32)
+            tail = accs[slot + 1, at, :] + precv_buf[2 * j + 1, at, :].astype(f32)
+            inverse = ss_send[at, :]
+            key = jnp.concatenate([lead[:, :half], tail[:, :half]], axis=1) * inverse + bias[0:1]
+            value = jnp.concatenate([lead[:, half:], tail[:, half:]], axis=1) * inverse + bias[1:2]
+            turned = jnp.concatenate([key[:, half:], key[:, :half]], axis=1)
+            kbuf[at, :] = (key * cos_ref[at, :] + turned * sin_ref[at, :]).astype(bf16)
+            vbuf[at, :] = value.astype(bf16)
+
+        scores = inner(qbuf[j], kbuf[...]) * scale
+        seen = lax.broadcasted_iota(jnp.int32, scores.shape, 1) < plen_ref[0]
+        scores = jnp.where(seen, scores, MASKED)
+        before = m_st[j][:, :1]
+        high = jnp.maximum(before, jnp.max(scores, axis=1, keepdims=True))
+        weights = jnp.exp(scores - high)
+        factor = jnp.exp(before - high)
+        mass = l_st[j][:, :1] * factor + jnp.sum(weights, axis=1, keepdims=True)
+        total = a_st[j] * factor + jnp.dot(
+            weights.astype(bf16), vbuf[...], preferred_element_type=f32
+        )
+        obuf[j] = (total / mass).astype(bf16)
+
+    def last_of(k, column):
+        slot = plane(k) * 2 + column
+        wait_all(slot, ox)
+        multiply(slot, ox, False)
+        complete(slot)
+
+    last_of(0, oy)
+    last_of(1, y)
+    wait_all(z * 2 + oy, ox)
+    multiply(z * 2 + oy, ox, False)
+    complete(z * 2 + oy)
+    last_of(1, oy)
+    finish(jnp.where(low, 0, 1))
+    last_of(2, y)
+    last_of(2, oy)
+    finish(jnp.where(low, 1, 0))
+
+    for j in range(heads):
+        for g in range(HEADS_PER_GROUP):
+            at = (j * HEADS_PER_GROUP + g) * HEAD_WIDTH
+            out_ref[:, at : at + HEAD_WIDTH] = obuf[j, g * fresh : (g + 1) * fresh, :]
+
+    for cond, copy in started:
+        if cond is None:
+            copy.wait_send()
+        else:
+            pl.when(cond)(copy.wait_send)
+    for copy in page_sends:
+        copy.wait_send()
+    for i in range(4):
+        part_copy(4 * ot + i).wait_send()
+
+
+def fused(
+    hidden, norm_gain, key_value_weight, key_value_bias, stored_page_pool, page_request, prefix_len,
+    queries, new_key_value,
+):
+    rows, width = hidden.shape
+    fresh = queries.shape[0]
+    pages, page_len = stored_page_pool.shape[:2]
+    cosine, sine = rotation_tables(rows)
+    vmem = pl.BlockSpec(memory_space=pltpu.VMEM)
+    smem = pl.BlockSpec(memory_space=pltpu.SMEM)
+    anywhere = pl.BlockSpec(memory_space=pl.ANY)
+    bf16, f32 = jnp.bfloat16, jnp.float32
+    dma = pltpu.SemaphoreType.DMA
+    return pl.pallas_call(
+        fused_kernel,
+        out_shape=jax.ShapeDtypeStruct(queries.shape, bf16),
+        in_specs=[anywhere, anywhere, vmem, vmem, vmem, smem, smem, vmem, vmem, vmem, vmem],
+        out_specs=vmem,
+        scratch_shapes=[
+            pltpu.VMEM((8, width, HEAD_WIDTH), bf16),
+            pltpu.VMEM((rows, width), bf16),
+            pltpu.VMEM((2, rows, width // 2), bf16),
+            pltpu.VMEM((8, rows, HEAD_WIDTH), f32),
+            pltpu.VMEM((4, rows, HEAD_WIDTH), bf16),
+            pltpu.VMEM((4, rows, HEAD_WIDTH), bf16),
+            pltpu.VMEM((rows, HEAD_WIDTH), f32),
+            pltpu.VMEM((rows, HEAD_WIDTH), f32),
+            pltpu.VMEM((8, page_len + FLAG_ROWS, 4 * HEAD_WIDTH), bf16),
+            pltpu.VMEM((8, page_len + FLAG_ROWS, 4 * HEAD_WIDTH), bf16),
+            pltpu.VMEM((2, HEADS_PER_GROUP * fresh, HEAD_WIDTH), bf16),
+            pltpu.VMEM((rows, HEAD_WIDTH), bf16),
+            pltpu.VMEM((rows, HEAD_WIDTH), bf16),
+            pltpu.VMEM((2, HEADS_PER_GROUP * fresh, HEAD_WIDTH), bf16),
+            pltpu.VMEM((2, HEADS_PER_GROUP * fresh, HEAD_WIDTH), f32),
+            pltpu.VMEM((2, HEADS_PER_GROUP * fresh, HEAD_WIDTH), f32),
+            pltpu.VMEM((2, HEADS_PER_GROUP * fresh, HEAD_WIDTH), f32),
+            dma((8,)), dma, dma,
+            dma((4, 8, 2, NSUB)), dma((8, 2, NSUB)),
+            dma((4,)), dma((4,)), dma((2,)), dma((8,)), dma((8,)),
+        ],
+        compiler_params=pltpu.CompilerParams(
+            collective_id=0, has_side_effects=True, vmem_limit_bytes=56 * 1024 * 1024
+        ),
+    )(
+        key_value_weight.reshape(width, HEAD_WIDTH),
+        hidden,
+        norm_gain.reshape(1, width),
+        key_value_bias,
+        stored_page_pool.reshape(pages, page_len, 4 * HEAD_WIDTH),
+        page_request,
+        prefix_len,
+        queries,
+        new_key_value.reshape(fresh, 4 * HEAD_WIDTH),
+        jnp.asarray(cosine),
+        jnp.asarray(sine),
+    )
+
+
 def solution(mesh):
+    shape = dict(mesh.shape)
+    small = shape["pool"] == 8 and shape["groups"] == 2 and shape["tensor"] == 2
     return jax.shard_map(
-        local,
+        fused if small else local,
         mesh=mesh,
         in_specs=(
             P(("groups", "pool"), "tensor"),

time: 221 us -> 125 us (0.57); the launches traced: 218 us -> 125 us
  waiting for transfers between devices: 146 us -> 0 us
  Pallas kernels: 0 us -> 116 us
  matrix products: 17.3 us -> 0 us
  between operations: 14.3 us -> 0.66 us
  other arithmetic: 13.6 us -> 0 us
  starting transfers between devices: 8.87 us -> 0 us
  local copies, waits for them, and re-layouts: 14.2 us -> 8.71 us
  blocking collectives: 3.7 us -> 0 us
    all_gather x1 -> x0, waiting for transfers between devices: 128 us -> none  [local(): piece = lax.all_gather(key_value_weight, 'pool', axis=2, tiled=True)]
    pallas_call x0 -> x1, Pallas kernels: none -> 116 us  [fused(): pl.pallas_call(fused_kernel, out_shape=jax.ShapeDtypeStruct(queries.shape...]
    dot_general x5 -> x0, matrix products: 17.3 us -> none  [the longest x1 14.8 us: local(): jnp.dot(scaled_scores, piece.reshape(piece.shape[0], 2 * width_part), pre...]
    all_to_all x2 -> x0, waiting for transfers between devices: 17 us -> none  [the longest x1 17 us: local(): lax.all_to_all(outgoing, 'pool', split_axis=0, concat_axis=0, tiled=True)]
    all_to_all x2 -> x0, starting transfers between devices: 8.83 us -> none  [the longest x1 5.52 us: local(): lax.all_to_all(outgoing, 'pool', split_axis=0, concat_axis=0, tiled=True)]
    reduce_sum x4 -> x0, other arithmetic: 6.29 us -> none  [the longest x1 5.07 us: local(): local_squares = jnp.sum(wide_hidden * wide_hidden, axis=1)]
    psum x1 -> x0, blocking collectives: 3.7 us -> none  [local(): squares = lax.psum(local_squares, 'tensor')]
    scatter x2 -> x0, local copies, waits for them, and re-layouts: 3.13 us -> none  [the longest x1 2.53 us: local(): outgoing = jnp.zeros((pool_size, CAP) + stored_page_pool.shape[1:], jnp.b...]
  transfers between devices with their start and end apart: 4 -> 0, of which waited for: 2 -> 0; matrix products, arithmetic and copies ran while one was open for 8% -> 0% of each run, Pallas kernels for 0% -> 0%
where the time goes in v1:
time: 125 us
  Pallas kernels  116 us (93%)
  local copies, waits for them, and re-layouts  8.71 us (7%)
    pallas_call x1, Pallas kernels, fused(): pl.pallas_call(fused_kernel, out_shape=jax.ShapeDtypeStruct(queries.shape...  116 us
    unnamed x2, local copies, waits for them, and re-layouts  2.95 us

profile of v1, /device:TPU:1, one launch (start us, length us, event | category | flops | bytes accessed | tf_op | source)
XLA Modules:
  0.0 125.1 jit_solution(5303155417874581111)
XLA Ops:
  0.7 1.3 %reshape.13.gain_ref = bf16[1,4096]{1,0:T(2,128)(2,1)} reshape(bf16[4096]{0:T(1024)(128)(2,1)} %param.12) | data formatting | bytes 16384 | tf_op jit(solution)/shard_map/reshape | solution.py:566
  2.0 1.4 %copy.14 = bf16[4,8,2,256]{3,1,2,0:T(8,128)(2,1)} copy(bf16[4,8,2,256]{3,2,1,0:T(2,128)(2,1)} %bitcast.5) | data formatting | bytes 65536
  3.3 2.2 %reshape.14.page_ref = bf16[4,128,512]{2,1,0:T(8,128)(2,1)} reshape(bf16[4,128,2,256]{3,2,1,0:T(2,128)(2,1)} %param.15) | data formatting | bytes 1048576 | tf_op jit(solution)/shard_map/reshape | solution.py:568
  5.5 2.3 %copy.13.w_ref = bf16[4096,128]{1,0:T(8,128)(2,1)} copy(bf16[4096,128]{0,1:T(8,128)(2,1)} %bitcast.3) | data formatting | bytes 2097152 | tf_op jit(solution)/shard_map/reshape | solution.py:564
  7.8 115.7 %shard_map.109 = bf16[32,2048]{1,0:T(8,128)(2,1)} custom-call(bf16[4096,128]{1,0:T(8,128)(2,1)} %copy.13.w_ref, bf16[1024,4096]{1,0:T(8,128)(2,1)} %h_ref.1, bf16[1,4096]{1,0:T(2,128)(2,1)} %reshape.13.gain_ref, bf16[2,256]{1,0:T(2,128)(2,1)} %bias_ref.1, bf16[4,128,512]{2,1,0:T(8,128)(2,1)} %reshape.14.page_ref, s32[4]{0:T(128)} %req_ref.1, ...), custom_call_target="tpu_custom_call" | custom-call | tf_op jit(solution)/shard_map/pallas_call | solution.py:533
  123.5 1.6 %copy.17 = bf16[32,2048]{1,0:T(8,128)(2,1)} copy(bf16[32,2048]{1,0:T(8,128)(2,1)} %shard_map.109) | data formatting | bytes 262144

commit v2 on v0

--- a/solution.py
+++ b/solution.py
@@ -1,8 +1,12 @@
+import functools
 import math
 
+import numpy as np
 import jax
 import jax.numpy as jnp
 from jax import lax
+from jax.experimental import pallas as pl
+from jax.experimental.pallas import tpu as pltpu
 from jax.sharding import PartitionSpec as P
 
 MODEL_WIDTH = 8192
@@ -13,6 +17,7 @@
 
 rope_base = 1000000.0
 epsilon = 1e-06
+MESH = pl.DeviceIdType.MESH
 
 
 def apply_rotation(key_portion, token_positions):
@@ -152,9 +157,471 @@
     return attended.transpose(2, 0, 1, 3).reshape(fresh_count, -1).astype(jnp.bfloat16)
 
 
+PIECES = 8
+ALONG_Z = 5
+ALONG_Y = 4
+PLANE_Y = 6
+REST_AT = 9
+PAGES_AT = 12
+FIRST_AT = 10
+AT_ONCE = (2, 2, 99, 99)
+MASKED = -1e30
+FLAG_ROWS = 16
+
+
+def rotation_tables(row_count):
+    half = HEAD_WIDTH // 2
+    frequency = rope_base ** (-(np.arange(half, dtype=np.float64) * 2.0 / HEAD_WIDTH))
+    angles = np.arange(row_count, dtype=np.float64)[:, None] * frequency[None, :]
+    cosine, sine = np.cos(angles), np.sin(angles)
+    return (
+        np.concatenate([cosine, cosine], axis=1).astype(np.float32),
+        np.concatenate([-sine, sine], axis=1).astype(np.float32),
+    )
+
+
+def fused_kernel(
+    w_ref, h_ref, gain_ref, bias_ref, page_ref, req_ref, plen_ref, q_ref, nkv_ref, cos_ref, sin_ref,
+    out_ref,
+    wbuf, hraw, hs, accs, psend_buf, precv_buf, ss_send, ss_recv, pout, pin, qbuf, kbuf, vbuf, obuf,
+    m_st, l_st, a_st, flat_pages,
+    h_sem, own_sem, page_self_sem, w_send, w_recv, part_send, part_recv, ss_sems, pg_send, pg_recv,
+):
+    f32, bf16 = jnp.float32, jnp.bfloat16
+    rows, sub = hs.shape[1], hs.shape[2]
+    x = lax.axis_index("groups")
+    me = lax.axis_index("pool")
+    t = lax.axis_index("tensor")
+    z, y = me // 2, lax.rem(me, 2)
+    ox, oy, ot = 1 - x, 1 - y, 1 - t
+    depth = 4
+
+    def device(g, p, c):
+        return {"groups": g, "pool": p, "tensor": c}
+
+    x_peer = device(ox, me, t)
+    y_peer = device(x, z * 2 + oy, t)
+    low = z < depth // 2
+    inside = (z > 0) & (z < depth - 1)
+    up, down = jnp.minimum(z + 1, depth - 1), jnp.maximum(z - 1, 0)
+    far_peer = device(x, jnp.where(low, up, down) * 2 + y, t)
+    near_peer = device(x, jnp.where(low, down, up) * 2 + y, t)
+    t_peer = device(x, me, ot)
+
+    blocks = h_sem.shape[0]
+    block_rows = rows // blocks
+
+    def hidden_copy(b):
+        window = pl.ds(b * block_rows, block_rows)
+        return pltpu.make_async_copy(h_ref.at[window], hraw.at[window], h_sem.at[b])
+
+    for b in range(blocks):
+        hidden_copy(b).start()
+    own_copies = [
+        pltpu.make_async_copy(w_ref.at[:, pl.ds(i * sub, sub)], wbuf.at[me, i], own_sem.at[i])
+        for i in range(PIECES)
+    ]
+    for copy in own_copies:
+        copy.start()
+
+    barrier = pltpu.get_barrier_semaphore()
+    for o in range(1, 8):
+        pl.semaphore_signal(
+            barrier, inc=1, device_id=device(x, lax.rem(me + o, 8), t), device_id_type=MESH
+        )
+    pl.semaphore_signal(barrier, inc=1, device_id=x_peer, device_id_type=MESH)
+    pl.semaphore_signal(barrier, inc=1, device_id=t_peer, device_id_type=MESH)
+    pl.semaphore_wait(barrier, 9)
+
+    def nth(r):
+        return jnp.where(x == 0, r, PIECES - 1 - r)
+
+    def copy_of(way, slot, r, peer):
+        piece = nth(r)
+        return pltpu.make_async_remote_copy(
+            src_ref=wbuf.at[slot, piece],
+            dst_ref=wbuf.at[slot, piece],
+            send_sem=w_send.at[way, slot, piece],
+            recv_sem=w_recv.at[slot, piece],
+            device_id=peer,
+            device_id_type=MESH,
+        )
+
+    in_flight = [[] for _ in AT_ONCE]
+
+    def run_if(cond, do):
+        if cond is None:
+            do()
+        else:
+            pl.when(cond)(do)
+
+    def send(way, slot, r, peer, cond=None):
+        queue = in_flight[way]
+        if len(queue) >= AT_ONCE[way]:
+            before, earlier = queue.pop(0)
+            run_if(before, earlier.wait_send)
+        copy = copy_of(way, slot, r, peer)
+        queue.append((cond, copy))
+        run_if(cond, copy.start)
+
+    def arrive(slot, r):
+        copy_of(2, slot, r, x_peer).wait_recv()
+
+    for copy in own_copies:
+        copy.wait()
+    def send_own(r):
+        send(1, me, r, near_peer, inside)
+        send(0, me, r, far_peer)
+
+    for r in range(2):
+        send_own(r)
+        if r < PIECES - PLANE_Y:
+            send(3, me, r, y_peer)
+
+    gain = gain_ref[...].astype(f32).reshape(1, PIECES * sub)
+
+    step_rows = 16
+
+    def scale_block(b):
+        hidden_copy(b).wait()
+
+        @pl.loop(0, block_rows // step_rows)
+        def _(i):
+            at = pl.ds(pl.multiple_of(b * block_rows + i * step_rows, step_rows), step_rows)
+            wide = hraw[at, :].astype(f32)
+            scaled = (wide * gain).astype(bf16)
+            for i in range(PIECES):
+                hs[i, at, :] = scaled[:, i * sub : (i + 1) * sub]
+            total = jnp.sum(wide * wide, axis=1, keepdims=True)
+            ss_send[at, :] = jnp.broadcast_to(total, (step_rows, HEAD_WIDTH))
+
+    mirrored = jnp.where(low, z, depth - 1 - z)
+
+    def plane(k):
+        o = 1 - mirrored if k == 0 else k + 1
+        return jnp.where(low, o, depth - 1 - o)
+
+    here_y, there_y = lambda k: plane(k) * 2 + y, lambda k: plane(k) * 2 + oy
+    plane_y = z * 2 + oy
+
+    def on_z(k, r):
+        slot = here_y(k)
+        arrive(slot, r)
+        if k > 0:
+            send(1, slot, r, near_peer, inside)
+        if r < ALONG_Y:
+            send(3, slot, r, y_peer)
+        if r < PIECES - ALONG_Z:
+            send(2, slot, r, x_peer)
+        if k == 0 and r + 2 < ALONG_Z:
+            send_own(r + 2)
+        if k == 1:
+            send(0, here_y(0), r, far_peer, inside)
+
+    def on_y(k, r):
+        slot = there_y(k)
+        arrive(slot, r)
+        send(2, slot, r, x_peer)
+
+    def on_plane(r):
+        arrive(plane_y, r)
+        send(2, plane_y, r, x_peer)
+
+    def multiply(p, pieces, first):
+        @pl.loop(0, rows // 256)
+        def _(b):
+            at = pl.ds(pl.multiple_of(b * 256, 256), 256)
+            total = None if first else accs[p, at, :]
+            for r in pieces:
+                shards = wbuf[pl.ds(p * 2, 2), nth(r)].reshape(2 * HEAD_WIDTH, sub)
+                part = lax.dot_general(
+                    hs[nth(r), at, :], shards, (((1,), (1,)), ((), ())), preferred_element_type=f32
+                )
+                total = part if total is None else total + part
+            accs[p, at, :] = total
+
+    def part_copy(p):
+        at = lax.rem(p, 2)
+        return pltpu.make_async_remote_copy(
+            src_ref=psend_buf.at[at],
+            dst_ref=precv_buf.at[at],
+            send_sem=part_send.at[at],
+            recv_sem=part_recv.at[at],
+            device_id=t_peer,
+            device_id_type=MESH,
+        )
+
+    def complete(p):
+        @pl.when(p // 2 != t)
+        def _():
+            psend_buf[lax.rem(p, 2)] = accs[p].astype(bf16)
+            part_copy(p).start()
+
+    page_len = page_ref.shape[1]
+    heads = 2
+    width = heads * HEAD_WIDTH
+
+    def pack(d):
+        taken = [(req_ref[i] == d).astype(f32) for i in range(page_ref.shape[0])]
+        for c in range(0, page_len, 32):
+            total = flat_pages[0, c : c + 32, :].astype(f32) * taken[0]
+            for i in range(1, page_ref.shape[0]):
+                total = total + flat_pages[i, c : c + 32, :].astype(f32) * taken[i]
+            pout[d, c : c + 32, :] = total.astype(bf16)
+        flag = sum(taken[1:], taken[0])
+        pout[d, page_len:, :] = (jnp.full((FLAG_ROWS, pout.shape[2]), 1.0, f32) * flag).astype(bf16)
+
+    def page_copy(o, source, target):
+        return pltpu.make_async_remote_copy(
+            src_ref=pout.at[target],
+            dst_ref=pin.at[source],
+            send_sem=pg_send.at[o],
+            recv_sem=pg_recv.at[o],
+            device_id=device(x, target, t),
+            device_id_type=MESH,
+        )
+
+    self_page = pltpu.make_async_copy(pout.at[me], pin.at[me], page_self_sem)
+    page_sends = [page_copy(o, me, lax.rem(me + o, 8)) for o in range(1, 8)]
+    ss_copy = pltpu.make_async_remote_copy(
+        src_ref=ss_send,
+        dst_ref=ss_recv,
+        send_sem=ss_sems.at[0],
+        recv_sem=ss_sems.at[1],
+        device_id=t_peer,
+        device_id_type=MESH,
+    )
+
+    def flatten(i):
+            for c in range(0, page_len, 32):
+                wide = page_ref[i, c : c + 32].astype(f32)
+                flat_pages[i, c : c + 32, :width] = wide[:, 0, :].astype(bf16)
+                flat_pages[i, c : c + 32, width:] = wide[:, 1, :].astype(bf16)
+
+    def send_pages():
+        self_page.start()
+        for copy in page_sends:
+            copy.start()
+
+    def rest_of_plane():
+        for r in range(PIECES - PLANE_Y, PLANE_Y):
+            send(3, me, r, y_peer)
+
+    beside = {}
+
+    def then(n, *work):
+        beside.setdefault(n, []).extend(work)
+
+    for b in range(blocks):
+        then(b, functools.partial(scale_block, b))
+    for i in range(page_ref.shape[0]):
+        then(i, functools.partial(flatten, i))
+    for d in range(8):
+        then(4 + d // 2, functools.partial(pack, d))
+    then(blocks, ss_copy.start)
+    then(REST_AT, rest_of_plane)
+    then(PAGES_AT, send_pages)
+    for i in range(4):
+        then(FIRST_AT + i, functools.partial(multiply, plane(0), (i,), i == 0))
+
+    for r in range(PIECES - PLANE_Y):
+        on_plane(r)
+    lag = 2
+    for n in range(3 * ALONG_Z + 3):
+        if n < 3 * ALONG_Z:
+            on_z(n // ALONG_Z, n % ALONG_Z)
+        k, r = (n - lag) // ALONG_Z, (n - lag) % ALONG_Z
+        if n >= lag and k < 3 and r < ALONG_Y:
+            on_y(k, r)
+        for work in beside.get(n, []):
+            work()
+
+    fresh = q_ref.shape[0]
+    group_rows = HEADS_PER_GROUP * fresh
+    scale = HEAD_WIDTH ** (-0.5)
+    for j in range(heads):
+        for g in range(HEADS_PER_GROUP):
+            at = (j * HEADS_PER_GROUP + g) * HEAD_WIDTH
+            qbuf[j, g * fresh : (g + 1) * fresh, :] = q_ref[:, at : at + HEAD_WIDTH]
+
+    def inner(a, b):
+        return lax.dot_general(a, b, (((1,), (1,)), ((), ())), preferred_element_type=f32)
+
+    def absorb(j, scores, values, first=False):
+        high = jnp.max(scores, axis=1, keepdims=True)
+        if not first:
+            before = m_st[j][:, :1]
+            high = jnp.maximum(before, high)
+        weights = jnp.exp(scores - high)
+        mass = jnp.broadcast_to(jnp.sum(weights, axis=1, keepdims=True), (group_rows, HEAD_WIDTH))
+        total = jnp.dot(weights.astype(bf16), values, preferred_element_type=f32)
+        if not first:
+            factor = jnp.exp(before - high)
+            mass = mass + l_st[j] * factor
+            total = total + a_st[j] * factor
+        m_st[j] = jnp.broadcast_to(high, (group_rows, HEAD_WIDTH))
+        l_st[j] = mass
+        a_st[j] = total
+
+    fresh_wide = nkv_ref[...].astype(f32)
+    new_keys, new_values = fresh_wide[:, 0, :].astype(bf16), fresh_wide[:, 1, :].astype(bf16)
+    for j in range(heads):
+        kc = j * HEAD_WIDTH
+        near = inner(qbuf[j], new_keys[:, kc : kc + HEAD_WIDTH]) * scale
+        row_at = lax.rem(lax.broadcasted_iota(jnp.int32, near.shape, 0), fresh)
+        near = jnp.where(lax.broadcasted_iota(jnp.int32, near.shape, 1) <= row_at, near, MASKED)
+        absorb(j, near, new_values[:, kc : kc + HEAD_WIDTH], True)
+
+    def pages_in():
+        self_page.wait()
+        for o in range(1, 8):
+            page_copy(o, lax.rem(me + 8 - o, 8), me).wait_recv()
+        flags = jnp.concatenate(
+            [pin[i, page_len:, :HEAD_WIDTH].astype(f32)[:1, :] for i in range(8)], axis=1
+        )
+        for j in range(heads):
+            kc, vc = j * HEAD_WIDTH, (heads + j) * HEAD_WIDTH
+            keys = pin[:, :page_len, kc : kc + HEAD_WIDTH].reshape(8 * page_len, HEAD_WIDTH)
+            values = pin[:, :page_len, vc : vc + HEAD_WIDTH].reshape(8 * page_len, HEAD_WIDTH)
+            absorb(j, jnp.where(flags > 0.5, inner(qbuf[j], keys) * scale, MASKED), values)
+
+    def norms():
+        ss_copy.wait()
+
+        @pl.loop(0, rows // 128)
+        def _(r):
+            at = pl.ds(pl.multiple_of(r * 128, 128), 128)
+            ss_send[at, :] = lax.rsqrt((ss_send[at, :] + ss_recv[at, :]) / MODEL_WIDTH + epsilon)
+
+    half = HEAD_WIDTH // 2
+
+    def finish(j):
+        p = 2 * t + j
+        part_copy(p).wait_recv()
+        bias = jnp.where(j == 0, bias_ref[:, :HEAD_WIDTH].astype(f32), bias_ref[:, HEAD_WIDTH:].astype(f32))
+
+        @pl.loop(0, rows // 128)
+        def _(r):
+            at = pl.ds(pl.multiple_of(r * 128, 128), 128)
+            both = accs[p, at, :] + precv_buf[j, at, :].astype(f32)
+            lead, tail = both[:, :HEAD_WIDTH], both[:, HEAD_WIDTH:]
+            inverse = ss_send[at, :]
+            key = jnp.concatenate([lead[:, :half], tail[:, :half]], axis=1) * inverse + bias[0:1]
+            value = jnp.concatenate([lead[:, half:], tail[:, half:]], axis=1) * inverse + bias[1:2]
+            turned = jnp.concatenate([key[:, half:], key[:, :half]], axis=1)
+            kbuf[at, :] = (key * cos_ref[at, :] + turned * sin_ref[at, :]).astype(bf16)
+            vbuf[at, :] = value.astype(bf16)
+
+        scores = inner(qbuf[j], kbuf[...]) * scale
+        seen = lax.broadcasted_iota(jnp.int32, scores.shape, 1) < plen_ref[0]
+        absorb(j, jnp.where(seen, scores, MASKED), vbuf[...])
+
+    def await_x(slot, first):
+        for r in range(PIECES - 1, first - 1, -1):
+            arrive(slot, r)
+
+    def close(k):
+        await_x(here_y(k), ALONG_Z)
+        await_x(there_y(k), ALONG_Y)
+        multiply(plane(k), range(ALONG_Y, PIECES), False)
+        complete(plane(k))
+
+    norms()
+    multiply(plane(1), range(ALONG_Y), True)
+    for r in range(PIECES - PLANE_Y, PLANE_Y):
+        arrive(plane_y, r)
+    multiply(z, range(PLANE_Y), True)
+    multiply(plane(2), range(ALONG_Y), True)
+    await_x(plane_y, PLANE_Y)
+    multiply(z, range(PLANE_Y, PIECES), False)
+    complete(z)
+    close(0)
+    close(1)
+    finish(jnp.where(low, 0, 1))
+    pages_in()
+    close(2)
+    finish(jnp.where(low, 1, 0))
+
+    for j in range(heads):
+        obuf[j] = (a_st[j] / l_st[j]).astype(bf16)
+    for j in range(heads):
+        for g in range(HEADS_PER_GROUP):
+            at = (j * HEADS_PER_GROUP + g) * HEAD_WIDTH
+            out_ref[:, at : at + HEAD_WIDTH] = obuf[j, g * fresh : (g + 1) * fresh, :]
+
+    for queue in in_flight:
+        for cond, copy in queue:
+            run_if(cond, copy.wait_send)
+    for copy in page_sends:
+        copy.wait_send()
+    for i in range(2):
+        part_copy(2 * ot + i).wait_send()
+
+
+def fused(
+    hidden, norm_gain, key_value_weight, key_value_bias, stored_page_pool, page_request, prefix_len,
+    queries, new_key_value,
+):
+    rows, width = hidden.shape
+    fresh = queries.shape[0]
+    pages, page_len = stored_page_pool.shape[:2]
+    cosine, sine = rotation_tables(rows)
+    vmem = pl.BlockSpec(memory_space=pltpu.VMEM)
+    smem = pl.BlockSpec(memory_space=pltpu.SMEM)
+    anywhere = pl.BlockSpec(memory_space=pl.ANY)
+    bf16, f32 = jnp.bfloat16, jnp.float32
+    dma = pltpu.SemaphoreType.DMA
+    return pl.pallas_call(
+        fused_kernel,
+        out_shape=jax.ShapeDtypeStruct(queries.shape, bf16),
+        in_specs=[anywhere, anywhere, vmem, vmem, vmem, smem, smem, vmem, vmem, vmem, vmem],
+        out_specs=vmem,
+        scratch_shapes=[
+            pltpu.VMEM((8, PIECES, HEAD_WIDTH, width // PIECES), bf16),
+            pltpu.VMEM((rows, width), bf16),
+            pltpu.VMEM((PIECES, rows, width // PIECES), bf16),
+            pltpu.VMEM((4, rows, 2 * HEAD_WIDTH), f32),
+            pltpu.VMEM((2, rows, 2 * HEAD_WIDTH), bf16),
+            pltpu.VMEM((2, rows, 2 * HEAD_WIDTH), bf16),
+            pltpu.VMEM((rows, HEAD_WIDTH), f32),
+            pltpu.VMEM((rows, HEAD_WIDTH), f32),
+            pltpu.VMEM((8, page_len + FLAG_ROWS, 4 * HEAD_WIDTH), bf16),
+            pltpu.VMEM((8, page_len + FLAG_ROWS, 4 * HEAD_WIDTH), bf16),
+            pltpu.VMEM((2, HEADS_PER_GROUP * fresh, HEAD_WIDTH), bf16),
+            pltpu.VMEM((rows, HEAD_WIDTH), bf16),
+            pltpu.VMEM((rows, HEAD_WIDTH), bf16),
+            pltpu.VMEM((2, HEADS_PER_GROUP * fresh, HEAD_WIDTH), bf16),
+            pltpu.VMEM((2, HEADS_PER_GROUP * fresh, HEAD_WIDTH), f32),
+            pltpu.VMEM((2, HEADS_PER_GROUP * fresh, HEAD_WIDTH), f32),
+            pltpu.VMEM((2, HEADS_PER_GROUP * fresh, HEAD_WIDTH), f32),
+            pltpu.VMEM((pages, page_len, 4 * HEAD_WIDTH), bf16),
+            dma((8,)), dma((PIECES,)), dma,
+            dma((4, 8, PIECES)), dma((8, PIECES)),
+            dma((2,)), dma((2,)), dma((2,)), dma((8,)), dma((8,)),
+        ],
+        compiler_params=pltpu.CompilerParams(
+            collective_id=0, has_side_effects=True, vmem_limit_bytes=56 * 1024 * 1024
+        ),
+    )(
+        key_value_weight.transpose(1, 2, 0).reshape(HEAD_WIDTH, width),
+        hidden,
+        norm_gain,
+        key_value_bias,
+        stored_page_pool,
+        page_request,
+        prefix_len,
+        queries,
+        new_key_value,
+        jnp.asarray(cosine),
+        jnp.asarray(sine),
+    )
+
+
 def solution(mesh):
+    shape = dict(mesh.shape)
+    small = shape["pool"] == 8 and shape["groups"] == 2 and shape["tensor"] == 2
     return jax.shard_map(
-        local,
+        fused if small else local,
         mesh=mesh,
         in_specs=(
             P(("groups", "pool"), "tensor"),

time: 221 us -> 106 us (0.48); the launches traced: 218 us -> 106 us
  waiting for transfers between devices: 146 us -> 0 us
  Pallas kernels: 0 us -> 104 us
  matrix products: 17.3 us -> 0 us
  between operations: 14.3 us -> 0.66 us
  other arithmetic: 13.6 us -> 0 us
  local copies, waits for them, and re-layouts: 14.2 us -> 1.57 us
  starting transfers between devices: 8.87 us -> 0 us
  blocking collectives: 3.7 us -> 0 us
    all_gather x1 -> x0, waiting for transfers between devices: 128 us -> none  [local(): piece = lax.all_gather(key_value_weight, 'pool', axis=2, tiled=True)]
    pallas_call x0 -> x1, Pallas kernels: none -> 104 us  [fused(): pl.pallas_call(fused_kernel, out_shape=jax.ShapeDtypeStruct(queries.shape...]
    dot_general x5 -> x0, matrix products: 17.3 us -> none  [the longest x1 14.8 us: local(): jnp.dot(scaled_scores, piece.reshape(piece.shape[0], 2 * width_part), pre...]
    all_to_all x2 -> x0, waiting for transfers between devices: 17 us -> none  [the longest x1 17 us: local(): lax.all_to_all(outgoing, 'pool', split_axis=0, concat_axis=0, tiled=True)]
    all_to_all x2 -> x0, starting transfers between devices: 8.83 us -> none  [the longest x1 5.52 us: local(): lax.all_to_all(outgoing, 'pool', split_axis=0, concat_axis=0, tiled=True)]
    reduce_sum x4 -> x0, other arithmetic: 6.29 us -> none  [the longest x1 5.07 us: local(): local_squares = jnp.sum(wide_hidden * wide_hidden, axis=1)]
    psum x1 -> x0, blocking collectives: 3.7 us -> none  [local(): squares = lax.psum(local_squares, 'tensor')]
    reshape x1 -> x0, local copies, waits for them, and re-layouts: 3.31 us -> none  [local(): kv_rows = kv_rows.reshape(row_count, 2, local_heads, HEAD_WIDTH)]
  transfers between devices with their start and end apart: 4 -> 0, of which waited for: 2 -> 0; matrix products, arithmetic and copies ran while one was open for 8% -> 0% of each run, Pallas kernels for 0% -> 0%
where the time goes in v2:
time: 106 us
  Pallas kernels  104 us (98%)
  local copies, waits for them, and re-layouts  1.57 us (1%)
    pallas_call x1, Pallas kernels, fused(): pl.pallas_call(fused_kernel, out_shape=jax.ShapeDtypeStruct(queries.shape...  104 us

profile of v2, /device:TPU:1, one launch (start us, length us, event | category | flops | bytes accessed | tf_op | source)
XLA Modules:
  0.0 106.1 jit_solution(1980957900242413679)
XLA Ops:
  0.7 103.8 %shard_map.109 = bf16[32,2048]{1,0:T(8,128)(2,1)} custom-call(bf16[128,4096]{1,0:T(8,128)(2,1)} %bitcast.3, bf16[1024,4096]{1,0:T(8,128)(2,1)} %h_ref.1, bf16[4096]{0:T(1024)(128)(2,1)} %gain_ref.1, bf16[2,256]{1,0:T(2,128)(2,1)} %bias_ref.1, bf16[4,128,2,256]{3,2,1,0:T(2,128)(2,1)} %page_ref.1, s32[4]{0:T(128)} %req_ref.1, s32[1]{0:T(128)S(6)} %copy.13.plen_ref, ...), custom_call_target="tpu_custom_call" | custom-call | tf_op jit(solution)/shard_map/pallas_call | solution.py:574
  104.5 1.6 %copy.14 = bf16[32,2048]{1,0:T(8,128)(2,1)} copy(bf16[32,2048]{1,0:T(8,128)(2,1)} %shard_map.109) | data formatting | bytes 262144

commit v3 on v2

--- a/solution.py
+++ b/solution.py
@@ -158,13 +158,13 @@
 
 
 PIECES = 8
-ALONG_Z = 5
+ALONG_Z = 4
 ALONG_Y = 4
 PLANE_Y = 6
-REST_AT = 9
-PAGES_AT = 12
-FIRST_AT = 10
-AT_ONCE = (2, 2, 99, 99)
+REST_AT = 13
+PAGES_AT = 13
+EARLY = 2
+AT_ONCE = (2, 2, 99, 3)
 MASKED = -1e30
 FLAG_ROWS = 16
 
@@ -231,52 +231,9 @@
         )
     pl.semaphore_signal(barrier, inc=1, device_id=x_peer, device_id_type=MESH)
     pl.semaphore_signal(barrier, inc=1, device_id=t_peer, device_id_type=MESH)
-    pl.semaphore_wait(barrier, 9)
-
-    def nth(r):
-        return jnp.where(x == 0, r, PIECES - 1 - r)
-
-    def copy_of(way, slot, r, peer):
-        piece = nth(r)
-        return pltpu.make_async_remote_copy(
-            src_ref=wbuf.at[slot, piece],
-            dst_ref=wbuf.at[slot, piece],
-            send_sem=w_send.at[way, slot, piece],
-            recv_sem=w_recv.at[slot, piece],
-            device_id=peer,
-            device_id_type=MESH,
-        )
-
-    in_flight = [[] for _ in AT_ONCE]
-
-    def run_if(cond, do):
-        if cond is None:
-            do()
-        else:
-            pl.when(cond)(do)
-
-    def send(way, slot, r, peer, cond=None):
-        queue = in_flight[way]
-        if len(queue) >= AT_ONCE[way]:
-            before, earlier = queue.pop(0)
-            run_if(before, earlier.wait_send)
-        copy = copy_of(way, slot, r, peer)
-        queue.append((cond, copy))
-        run_if(cond, copy.start)
-
-    def arrive(slot, r):
-        copy_of(2, slot, r, x_peer).wait_recv()
-
-    for copy in own_copies:
-        copy.wait()
-    def send_own(r):
-        send(1, me, r, near_peer, inside)
-        send(0, me, r, far_peer)
-
-    for r in range(2):
-        send_own(r)
-        if r < PIECES - PLANE_Y:
-            send(3, me, r, y_peer)
+    page_len = page_ref.shape[1]
+    heads = 2
+    width = heads * HEAD_WIDTH
 
     gain = gain_ref[...].astype(f32).reshape(1, PIECES * sub)
 
@@ -294,147 +251,6 @@
                 hs[i, at, :] = scaled[:, i * sub : (i + 1) * sub]
             total = jnp.sum(wide * wide, axis=1, keepdims=True)
             ss_send[at, :] = jnp.broadcast_to(total, (step_rows, HEAD_WIDTH))
-
-    mirrored = jnp.where(low, z, depth - 1 - z)
-
-    def plane(k):
-        o = 1 - mirrored if k == 0 else k + 1
-        return jnp.where(low, o, depth - 1 - o)
-
-    here_y, there_y = lambda k: plane(k) * 2 + y, lambda k: plane(k) * 2 + oy
-    plane_y = z * 2 + oy
-
-    def on_z(k, r):
-        slot = here_y(k)
-        arrive(slot, r)
-        if k > 0:
-            send(1, slot, r, near_peer, inside)
-        if r < ALONG_Y:
-            send(3, slot, r, y_peer)
-        if r < PIECES - ALONG_Z:
-            send(2, slot, r, x_peer)
-        if k == 0 and r + 2 < ALONG_Z:
-            send_own(r + 2)
-        if k == 1:
-            send(0, here_y(0), r, far_peer, inside)
-
-    def on_y(k, r):
-        slot = there_y(k)
-        arrive(slot, r)
-        send(2, slot, r, x_peer)
-
-    def on_plane(r):
-        arrive(plane_y, r)
-        send(2, plane_y, r, x_peer)
-
-    def multiply(p, pieces, first):
-        @pl.loop(0, rows // 256)
-        def _(b):
-            at = pl.ds(pl.multiple_of(b * 256, 256), 256)
-            total = None if first else accs[p, at, :]
-            for r in pieces:
-                shards = wbuf[pl.ds(p * 2, 2), nth(r)].reshape(2 * HEAD_WIDTH, sub)
-                part = lax.dot_general(
-                    hs[nth(r), at, :], shards, (((1,), (1,)), ((), ())), preferred_element_type=f32
-                )
-                total = part if total is None else total + part
-            accs[p, at, :] = total
-
-    def part_copy(p):
-        at = lax.rem(p, 2)
-        return pltpu.make_async_remote_copy(
-            src_ref=psend_buf.at[at],
-            dst_ref=precv_buf.at[at],
-            send_sem=part_send.at[at],
-            recv_sem=part_recv.at[at],
-            device_id=t_peer,
-            device_id_type=MESH,
-        )
-
-    def complete(p):
-        @pl.when(p // 2 != t)
-        def _():
-            psend_buf[lax.rem(p, 2)] = accs[p].astype(bf16)
-            part_copy(p).start()
-
-    page_len = page_ref.shape[1]
-    heads = 2
-    width = heads * HEAD_WIDTH
-
-    def pack(d):
-        taken = [(req_ref[i] == d).astype(f32) for i in range(page_ref.shape[0])]
-        for c in range(0, page_len, 32):
-            total = flat_pages[0, c : c + 32, :].astype(f32) * taken[0]
-            for i in range(1, page_ref.shape[0]):
-                total = total + flat_pages[i, c : c + 32, :].astype(f32) * taken[i]
-            pout[d, c : c + 32, :] = total.astype(bf16)
-        flag = sum(taken[1:], taken[0])
-        pout[d, page_len:, :] = (jnp.full((FLAG_ROWS, pout.shape[2]), 1.0, f32) * flag).astype(bf16)
-
-    def page_copy(o, source, target):
-        return pltpu.make_async_remote_copy(
-            src_ref=pout.at[target],
-            dst_ref=pin.at[source],
-            send_sem=pg_send.at[o],
-            recv_sem=pg_recv.at[o],
-            device_id=device(x, target, t),
-            device_id_type=MESH,
-        )
-
-    self_page = pltpu.make_async_copy(pout.at[me], pin.at[me], page_self_sem)
-    page_sends = [page_copy(o, me, lax.rem(me + o, 8)) for o in range(1, 8)]
-    ss_copy = pltpu.make_async_remote_copy(
-        src_ref=ss_send,
-        dst_ref=ss_recv,
-        send_sem=ss_sems.at[0],
-        recv_sem=ss_sems.at[1],
-        device_id=t_peer,
-        device_id_type=MESH,
-    )
-
-    def flatten(i):
-            for c in range(0, page_len, 32):
-                wide = page_ref[i, c : c + 32].astype(f32)
-                flat_pages[i, c : c + 32, :width] = wide[:, 0, :].astype(bf16)
-                flat_pages[i, c : c + 32, width:] = wide[:, 1, :].astype(bf16)
-
-    def send_pages():
-        self_page.start()
-        for copy in page_sends:
-            copy.start()
-
-    def rest_of_plane():
-        for r in range(PIECES - PLANE_Y, PLANE_Y):
-            send(3, me, r, y_peer)
-
-    beside = {}
-
-    def then(n, *work):
-        beside.setdefault(n, []).extend(work)
-
-    for b in range(blocks):
-        then(b, functools.partial(scale_block, b))
-    for i in range(page_ref.shape[0]):
-        then(i, functools.partial(flatten, i))
-    for d in range(8):
-        then(4 + d // 2, functools.partial(pack, d))
-    then(blocks, ss_copy.start)
-    then(REST_AT, rest_of_plane)
-    then(PAGES_AT, send_pages)
-    for i in range(4):
-        then(FIRST_AT + i, functools.partial(multiply, plane(0), (i,), i == 0))
-
-    for r in range(PIECES - PLANE_Y):
-        on_plane(r)
-    lag = 2
-    for n in range(3 * ALONG_Z + 3):
-        if n < 3 * ALONG_Z:
-            on_z(n // ALONG_Z, n % ALONG_Z)
-        k, r = (n - lag) // ALONG_Z, (n - lag) % ALONG_Z
-        if n >= lag and k < 3 and r < ALONG_Y:
-            on_y(k, r)
-        for work in beside.get(n, []):
-            work()
 
     fresh = q_ref.shape[0]
     group_rows = HEADS_PER_GROUP * fresh
@@ -472,6 +288,206 @@
         near = jnp.where(lax.broadcasted_iota(jnp.int32, near.shape, 1) <= row_at, near, MASKED)
         absorb(j, near, new_values[:, kc : kc + HEAD_WIDTH], True)
 
+    for b in range(EARLY):
+        scale_block(b)
+    pl.semaphore_wait(barrier, 9)
+
+    def nth(r):
+        return jnp.where(x == 0, r, PIECES - 1 - r)
+
+    def copy_of(way, slot, r, peer):
+        piece = nth(r)
+        return pltpu.make_async_remote_copy(
+            src_ref=wbuf.at[slot, piece],
+            dst_ref=wbuf.at[slot, piece],
+            send_sem=w_send.at[way, slot, piece],
+            recv_sem=w_recv.at[slot, piece],
+            device_id=peer,
+            device_id_type=MESH,
+        )
+
+    in_flight = [[] for _ in AT_ONCE]
+
+    def run_if(cond, do):
+        if cond is None:
+            do()
+        else:
+            pl.when(cond)(do)
+
+    def send(way, slot, r, peer, cond=None):
+        queue = in_flight[way]
+        if len(queue) >= AT_ONCE[way]:
+            before, earlier = queue.pop(0)
+            run_if(before, earlier.wait_send)
+        copy = copy_of(way, slot, r, peer)
+        queue.append((cond, copy))
+        run_if(cond, copy.start)
+
+    def arrive(slot, r):
+        copy_of(2, slot, r, x_peer).wait_recv()
+
+    for copy in own_copies:
+        copy.wait()
+    def send_own(r):
+        send(1, me, r, near_peer, inside)
+        send(0, me, r, far_peer)
+
+    for r in range(2):
+        send_own(r)
+        if r < PIECES - PLANE_Y:
+            send(3, me, r, y_peer)
+
+    mirrored = jnp.where(low, z, depth - 1 - z)
+
+    def plane(k):
+        o = 1 - mirrored if k == 0 else k + 1
+        return jnp.where(low, o, depth - 1 - o)
+
+    here_y, there_y = lambda k: plane(k) * 2 + y, lambda k: plane(k) * 2 + oy
+    plane_y = z * 2 + oy
+
+    def on_z(k, r):
+        slot = here_y(k)
+        arrive(slot, r)
+        if k > 0:
+            send(1, slot, r, near_peer, inside)
+        if r < ALONG_Y:
+            send(3, slot, r, y_peer)
+        if r < PIECES - ALONG_Z:
+            send(2, slot, r, x_peer)
+        if k == 0 and r + 2 < ALONG_Z:
+            send_own(r + 2)
+        if k == 1:
+            send(0, here_y(0), r, far_peer, inside)
+
+    def on_y(k, r):
+        slot = there_y(k)
+        arrive(slot, r)
+        send(2, slot, r, x_peer)
+
+    def on_plane(r):
+        arrive(plane_y, r)
+        send(2, plane_y, r, x_peer)
+
+    def multiply(p, pieces, first):
+        @pl.loop(0, rows // 256)
+        def _(b):
+            at = pl.ds(pl.multiple_of(b * 256, 256), 256)
+            total = None if first else accs[p, at, :]
+            for r in pieces:
+                shards = wbuf[pl.ds(p * 2, 2), nth(r)].reshape(2 * HEAD_WIDTH, sub)
+                part = lax.dot_general(
+                    hs[nth(r), at, :], shards, (((1,), (1,)), ((), ())), preferred_element_type=f32
+                )
+                total = part if total is None else total + part
+            accs[p, at, :] = total
+
+    def part_copy(p):
+        at = lax.rem(p, 2)
+        return pltpu.make_async_remote_copy(
+            src_ref=psend_buf.at[at],
+            dst_ref=precv_buf.at[at],
+            send_sem=part_send.at[at],
+            recv_sem=part_recv.at[at],
+            device_id=t_peer,
+            device_id_type=MESH,
+        )
+
+    def complete(p):
+        @pl.when(p // 2 != t)
+        def _():
+            psend_buf[lax.rem(p, 2)] = accs[p].astype(bf16)
+            part_copy(p).start()
+
+
+    def pack(d):
+        taken = [(req_ref[i] == d).astype(f32) for i in range(page_ref.shape[0])]
+        picks = [(jnp.zeros((32, 2 * width), f32) + one).astype(bf16) for one in taken]
+        for c in range(0, page_len, 32):
+            total = flat_pages[0, c : c + 32, :] * picks[0]
+            for i in range(1, page_ref.shape[0]):
+                total = total + flat_pages[i, c : c + 32, :] * picks[i]
+            pout[d, c : c + 32, :] = total
+        flag = sum(taken[1:], taken[0])
+        pout[d, page_len:, :] = (jnp.full((FLAG_ROWS, pout.shape[2]), 1.0, f32) * flag).astype(bf16)
+
+    def page_copy(o, source, target):
+        return pltpu.make_async_remote_copy(
+            src_ref=pout.at[target],
+            dst_ref=pin.at[source],
+            send_sem=pg_send.at[o],
+            recv_sem=pg_recv.at[o],
+            device_id=device(x, target, t),
+            device_id_type=MESH,
+        )
+
+    self_page = pltpu.make_async_copy(pout.at[me], pin.at[me], page_self_sem)
+    page_sends = [page_copy(o, me, lax.rem(me + o, 8)) for o in range(1, 8)]
+    ss_copy = pltpu.make_async_remote_copy(
+        src_ref=ss_send,
+        dst_ref=ss_recv,
+        send_sem=ss_sems.at[0],
+        recv_sem=ss_sems.at[1],
+        device_id=t_peer,
+        device_id_type=MESH,
+    )
+
+    def flatten(i):
+            for c in range(0, page_len, 32):
+                wide = page_ref[i, c : c + 32].astype(f32)
+                flat_pages[i, c : c + 32, :width] = wide[:, 0, :].astype(bf16)
+                flat_pages[i, c : c + 32, width:] = wide[:, 1, :].astype(bf16)
+
+    def send_pages():
+        self_page.start()
+        for copy in page_sends:
+            copy.start()
+
+    def rest_of_plane():
+        for r in range(PIECES - PLANE_Y, PLANE_Y):
+            send(3, me, r, y_peer)
+
+    def norms():
+        ss_copy.wait()
+
+        @pl.loop(0, rows // 128)
+        def _(r):
+            at = pl.ds(pl.multiple_of(r * 128, 128), 128)
+            ss_send[at, :] = lax.rsqrt((ss_send[at, :] + ss_recv[at, :]) / MODEL_WIDTH + epsilon)
+
+    beside = {}
+
+    def then(n, *work):
+        beside.setdefault(n, []).extend(work)
+
+    for b in range(EARLY, blocks):
+        then(b - EARLY, functools.partial(scale_block, b))
+    for i in range(page_ref.shape[0]):
+        then(i, functools.partial(flatten, i))
+    for d in range(8):
+        then(4 + d // 2, functools.partial(pack, d))
+    then(blocks - EARLY, ss_copy.start)
+    then(REST_AT, rest_of_plane)
+    then(PAGES_AT, send_pages)
+    for i in range(4):
+        then(8 + i, functools.partial(multiply, plane(0), (i,), i == 0))
+        then(12 + i, functools.partial(multiply, plane(1), (i,), i == 0))
+    then(14, norms)
+    then(16, functools.partial(multiply, plane(2), (0, 1), True))
+    then(17, functools.partial(multiply, plane(2), (2, 3), False))
+
+    for r in range(PIECES - PLANE_Y):
+        on_plane(r)
+    lag = 2
+    for n in range(18):
+        if n < 3 * ALONG_Z:
+            on_z(n // ALONG_Z, n % ALONG_Z)
+        k, r = (n - lag) // ALONG_Z, (n - lag) % ALONG_Z
+        if n >= lag and k < 3 and r < ALONG_Y:
+            on_y(k, r)
+        for work in beside.get(n, []):
+            work()
+
     def pages_in():
         self_page.wait()
         for o in range(1, 8):
@@ -485,14 +501,6 @@
             values = pin[:, :page_len, vc : vc + HEAD_WIDTH].reshape(8 * page_len, HEAD_WIDTH)
             absorb(j, jnp.where(flags > 0.5, inner(qbuf[j], keys) * scale, MASKED), values)
 
-    def norms():
-        ss_copy.wait()
-
-        @pl.loop(0, rows // 128)
-        def _(r):
-            at = pl.ds(pl.multiple_of(r * 128, 128), 128)
-            ss_send[at, :] = lax.rsqrt((ss_send[at, :] + ss_recv[at, :]) / MODEL_WIDTH + epsilon)
-
     half = HEAD_WIDTH // 2
 
     def finish(j):
@@ -526,12 +534,9 @@
         multiply(plane(k), range(ALONG_Y, PIECES), False)
         complete(plane(k))
 
-    norms()
-    multiply(plane(1), range(ALONG_Y), True)
     for r in range(PIECES - PLANE_Y, PLANE_Y):
         arrive(plane_y, r)
     multiply(z, range(PLANE_Y), True)
-    multiply(plane(2), range(ALONG_Y), True)
     await_x(plane_y, PLANE_Y)
     multiply(z, range(PLANE_Y, PIECES), False)
     complete(z)

time: 106 us -> 99 us (0.934)
  Pallas kernels: 104 us -> 96.6 us
    pallas_call x1, Pallas kernels: 104 us -> 96.6 us  [fused(): pl.pallas_call(fused_kernel, out_shape=jax.ShapeDtypeStruct(queries.shape...]
where the time goes in v3:
time: 99 us; the launch traced here: 98.8 us
  Pallas kernels  96.6 us (98%)
  local copies, waits for them, and re-layouts  1.57 us (2%)
    pallas_call x1, Pallas kernels, fused(): pl.pallas_call(fused_kernel, out_shape=jax.ShapeDtypeStruct(queries.shape...  96.6 us

profile of v3, /device:TPU:1, one launch (start us, length us, event | category | flops | bytes accessed | tf_op | source)
XLA Modules:
  0.0 98.8 jit_solution(4658418908198577175)
XLA Ops:
  0.7 96.6 %shard_map.109 = bf16[32,2048]{1,0:T(8,128)(2,1)} custom-call(bf16[128,4096]{1,0:T(8,128)(2,1)} %bitcast.3, bf16[1024,4096]{1,0:T(8,128)(2,1)} %h_ref.1, bf16[4096]{0:T(1024)(128)(2,1)} %gain_ref.1, bf16[2,256]{1,0:T(2,128)(2,1)} %bias_ref.1, bf16[4,128,2,256]{3,2,1,0:T(2,128)(2,1)} %page_ref.1, s32[4]{0:T(128)} %req_ref.1, s32[1]{0:T(128)S(6)} %copy.13.plen_ref, ...), custom_call_target="tpu_custom_call" | custom-call | tf_op jit(solution)/shard_map/pallas_call | solution.py:579
  97.2 1.6 %copy.14 = bf16[32,2048]{1,0:T(8,128)(2,1)} copy(bf16[32,2048]{1,0:T(8,128)(2,1)} %shard_map.109) | data formatting | bytes 262144
